TPU v7x, 32 devices: a whole 2x2x4 slice. The times are simulated.
32 devices in a mesh: groups: 2 (over x), ctx: 16 (over z, y, core).
Axes of the slice: x: 2, y: 2, z: 4, core: 2. Of those that a mesh axis runs over, the one named last changes fastest.
Arguments:
- query_rows: bfloat16 [8192, 4096], P(('groups', 'ctx')), parts along dimension 0, may hold values from -6 to 6
- key_rows: bfloat16 [8192, 4096], P(('groups', 'ctx')), parts along dimension 0, may hold values from -6 to 6
- value_rows: bfloat16 [8192, 4096], P(('groups', 'ctx')), parts along dimension 0, may hold values from -45 to 45
- out_gain: float32 [4096], replicated, may hold values from 0.25 to 1.75
Outputs:
- attended: bfloat16 [8192, 4096], P(('groups', 'ctx')), parts along dimension 0
- final_state: float32 [8192, 128], P(('groups', 'ctx')), parts along dimension 0
There are 2 independent parts, one for each index of `groups`. A program takes and returns all parts, laid end to end along the dimension named above; an argument that names none is the same for every part. Nothing has to cross between parts.
All inputs are finite; a program needn't handle non-finite values.
Results may differ from a plain program's by a relative error of at most 0.0051.
Values sent between devices are 32-bit elements; how exact they have to be, the bound alone decides.
A program may use at most 320 MiB of HBM per device.

v0:
```python
import jax
import jax.numpy as jnp
from jax import lax
from jax.sharding import PartitionSpec as P

H = 32
DH = 128
BLK = 128


def entering(shard, axis, combine, identity):
    length, mine = (lax.axis_size(axis), lax.axis_index(axis))
    everything = lax.all_gather(shard, axis)
    start = jnp.broadcast_to(jnp.asarray(identity, shard.dtype), shard.shape)

    def lap(k, before):
        reached = k < mine
        new = combine(before, everything[k])
        return jnp.where(reached, new, before)

    return lax.fori_loop(0, length, lap, start)


def add_states(earlier, later):
    return earlier + later


def silu_round(values):
    return jax.nn.silu(values.astype(jnp.float32)).astype(jnp.bfloat16)


def shards(query_rows, key_rows, value_rows, out_gain):
    tok_rows = query_rows.shape[0]
    blocks = tok_rows // BLK
    feat_q = silu_round(query_rows).reshape(blocks, BLK, H, DH)
    feat_k = silu_round(key_rows).reshape(blocks, BLK, H, DH)
    values = value_rows.reshape(blocks, BLK, H, DH)
    causal = jnp.arange(BLK)[:, None] >= jnp.arange(BLK)[None, :]
    scores = jnp.einsum("cihd,cjhd->chij", feat_q, feat_k, preferred_element_type=jnp.float32)
    scores = jnp.where(causal[None, None], scores, jnp.float32(0.0)).astype(jnp.bfloat16)
    intra = jnp.einsum("chij,cjhd->cihd", scores, values, preferred_element_type=jnp.float32)
    block_state = jnp.einsum("cjhd,cjhe->chde", feat_k, values, preferred_element_type=jnp.float32)
    running = jnp.cumsum(block_state, axis=0)
    local_before = running - block_state
    total = running[-1]
    seq_len = tok_rows * lax.axis_size("ctx")
    prefix = entering(total, "ctx", add_states, jnp.zeros_like(total))
    carried = (prefix[None] + local_before).astype(jnp.bfloat16)
    inter = jnp.einsum("cihd,chde->cihe", feat_q, carried, preferred_element_type=jnp.float32)
    summed = lax.psum_scatter(total.reshape(H * DH, DH), "ctx", scatter_dimension=0, tiled=True)
    final_state = summed * seq_len ** (-0.5)
    mixed = (intra + inter).reshape(tok_rows, H * DH)
    scale = lax.rsqrt(jnp.mean(mixed * mixed, axis=1, keepdims=True) + 1e-05)
    attended = (mixed * scale * out_gain[None, :]).astype(jnp.bfloat16)
    return (attended, final_state)


def solution(mesh):
    return jax.shard_map(
        shards,
        mesh=mesh,
        in_specs=(
            P(("groups", "ctx"), None),
            P(("groups", "ctx"), None),
            P(("groups", "ctx"), None),
            P(),
        ),
        out_specs=(P(("groups", "ctx"), None), P(("groups", "ctx"), None)),
        check_vma=False,
    )
```

profile of v0, /device:TPU:25, one launch (start us, length us, event | category | flops | bytes accessed | tf_op | source)
XLA Modules:
  0.0 323.5 jit_solution(1171005859967154366)
XLA Ops:
  7.2 0.0 reduce-scatter.2.cloned.1.call-start
  7.2 2.7 fusion.10
  9.9 1.8 copy.27
  11.7 3.5 %copy.20 = bf16[2,128,32,128]{1,3,2,0:T(8,128)(2,1)S(1)} copy(bf16[2,128,32,128]{3,2,1,0:T(8,128)(2,1)} %bitcast.39) | data formatting | bytes 4194304 | tf_op jit(solution)/shard_map/reshape | solution.py:36
  15.2 0.0 copy-start.2
  15.2 2.8 copy.28
  18.0 0.0 copy-start.3
  18.0 0.0 copy-done.2
  18.0 1.3 copy-done.3
  19.4 1.5 fusion.15
  20.8 0.0 copy-start
  20.8 1.9 fusion.22
  22.7 0.0 copy-done
  22.8 0.0 copy-start.1
  22.8 2.1 copy-done.1
  24.8 1.5 slice.4
  26.3 0.0 reduce-scatter.2.cloned.1.call-update
  26.3 0.2 all-gather.2.cloned.1.call-start
  26.6 0.5 all-gather.2.cloned.1.call-update
  27.1 2.7 fusion.11
  29.8 1.8 copy.26
  31.6 7.6 %fusion.13 = f32[2,32,128,128]{2,3,1,0:T(8,128)} fusion(bf16[2,128,32,128]{3,2,1,0:T(8,128)(2,1)} %bitcast.35, bf16[2,128,32,128]{1,3,2,0:T(8,128)(2,1)} %copy-done.2, pred[128,128]{1,0:T(8,128)(4,1)S(1)} %iota_compare_fusion, bf16[2,128,32,128]{3,2,1,0:T(8,128)(2,1)} %bitcast.36), kind=kOutput, calls=%fused_computation.23 | convolution fusion | flops 538968064 | bytes 10502144 | tf_op jit(solution)/shard_map/chij,cjhd->cihd/dot_general | solution.py:41
  39.2 47.1 %reduce-scatter.2.cloned.1.call-done = f32[256,128]{1,0:T(8,128)} async-done(((f32[4096,128]{1,0:T(8,128)}), f32[256,128]{1,0:T(8,128)}) %reduce-scatter.2.cloned.1.call-update) | async-done | bytes 131088 | tf_op jit(solution)/shard_map/reduce_scatter | solution.py:50
  86.3 1.6 broadcast_multiply_fusion
  87.9 170.4 %all-gather.2.cloned.1.call-done = f32[16,32,128,128]{3,2,1,0:T(8,128)} async-done(((f32[1,32,128,128]{3,2,1,0:T(8,128)}), f32[16,32,128,128]{3,2,1,0:T(8,128)}) %all-gather.2.cloned.1.call-update) | async-done | bytes 33554448 | tf_op jit(solution)/shard_map/all_gather | solution.py:13
  258.3 37.3 %while.14 = (s32[]{:T(128)}, f32[32,128,128]{2,1,0:T(8,128)S(1)}, s32[]{:T(128)}, f32[16,32,128,128]{3,2,1,0:T(8,128)}, s32[]{:T(128)}, /*index=5*/s32[]{:T(128)}) while((s32[]{:T(128)}, f32[32,128,128]{2,1,0:T(8,128)S(1)}, s32[]{:T(128)}, f32[16,32,128,128]{3,2,1,0:T(8,128)}, s32[]{:T(128)}, /*index=5*/s32[]{:T(128)}) %tuple.37), condition=%wide.region_2.3_spmd.clone, body=%wide.region_1.2_spmd.clone.sunk | while | flops 1572868 | bytes 6291549 | solution.py:21
  258.3 2.3 add_select_fusion.2
  260.6 2.3 add_select_fusion.2
  262.9 2.3 add_select_fusion.2
  265.3 2.3 add_select_fusion.2
  267.6 2.3 add_select_fusion.2
  269.9 2.3 add_select_fusion.2
  272.3 2.3 add_select_fusion.2
  274.6 2.3 add_select_fusion.2
  276.9 2.3 add_select_fusion.2
  279.3 2.3 add_select_fusion.2
  281.6 2.3 add_select_fusion.2
  284.0 2.3 add_select_fusion.2
  286.3 2.3 add_select_fusion.2
  288.6 2.3 add_select_fusion.2
  291.0 2.3 add_select_fusion.2
  293.3 2.3 add_select_fusion.2
  295.6 9.0 %multiply_reduce_fusion = (f32[2,128]{1,0:T(2,128)S(1)}, f32[2,128,32,128]{1,3,2,0:T(8,128)}) fusion(bf16[2,128,32,128]{3,2,1,0:T(8,128)(2,1)} %bitcast.37, f32[2,32,128,128]{3,2,1,0:T(8,128)} %copy-done.1, f32[2,32,128,128]{3,2,1,0:T(8,128)} %copy-done, f32[32,128,128]{2,1,0:T(8,128)S(1)} %get-tuple-element.81, f32[2,32,128,128]{2,3,1,0:T(8,128)} %fusion.13), kind=kOutput, calls=%fused_computation.17 | convolution fusion | flops 274726656 | bytes 20972544 | tf_op jit(solution)/shard_map/cihd,chde->cihe/dot_general | solution.py:49
  304.7 0.0 copy-start.4
  304.7 5.5 %copy.24 = f32[2,128,32,128]{3,2,1,0:T(8,128)} copy(f32[2,128,32,128]{1,3,2,0:T(8,128)} %get-tuple-element.106) | data formatting | bytes 8388608 | tf_op jit(solution)/shard_map/add | solution.py:52
  310.2 0.0 copy-done.4
  310.2 6.5 %fusion.9 = bf16[256,4096]{1,0:T(8,128)(2,1)} fusion(f32[32,8,32,128]{3,2,1,0:T(8,128)} %bitcast.38, f32[4096]{0:T(1024)S(1)} %copy-done.4, f32[256]{0:T(256)S(1)} %rsqrt_bitcast_fusion), kind=kLoop, calls=%fused_computation.15 | loop fusion | flops 3145728 | bytes 6308864 | tf_op jit(solution)/shard_map/convert_element_type | solution.py:54
  (3 shorter events, 0.0 us)
Async XLA Ops:
  7.2 79.1 %reduce-scatter.2.cloned.1.call-start = ((), (), s32[]{:S(2)}) async-start(), calls=%async_computation.2 | async-start | bytes 2228224 | tf_op jit(solution)/shard_map/reduce_scatter | solution.py:50
  15.2 2.9 copy-start.2
  18.0 1.3 copy-start.3
  20.8 2.0 copy-start
  22.8 2.1 copy-start.1
  26.3 231.9 %all-gather.2.cloned.1.call-start = ((), (), s32[]{:S(2)}) async-start(), calls=%async_computation.1 | async-start | bytes 35651584 | tf_op jit(solution)/shard_map/all_gather | solution.py:13
  304.7 5.5 %copy-start.4 = (f32[4096]{0:T(1024)S(1)}, f32[4096]{0:T(1024)}, u32[]{:S(2)}) copy-start(f32[4096]{0:T(1024)} %param.9) | copy-start | bytes 49156
Sparse Core Ops, SparseCore 0:
  26.5 59.7 reduce-scatter.1
  88.0 170.2 all-gather.1
where the time goes:
time: 326 us; the launch traced here: 323 us
  waiting for transfers between devices  218 us (67%)
  other arithmetic  52.3 us (16%)
  local copies, waits for them, and re-layouts  20.3 us (6%)
  matrix products  18.1 us (6%)
  between operations  14.1 us (4%)
    all_gather x1, waiting for transfers between devices, entering(): everything = lax.all_gather(shard, axis)  170 us
    reduce_scatter x1, waiting for transfers between devices, shards(): lax.psum_scatter(total.reshape(H * DH, DH), 'ctx', scatter_dimension=0, t...  47.1 us
    select_n x16, other arithmetic, lap(): return jnp.where(reached, new, before)  37 us
    unnamed x13, local copies, waits for them, and re-layouts  9.87 us
    dot_general x1, matrix products, shards(): jnp.einsum('cihd,chde->cihe', feat_q, carried, preferred_element_type=jnp...  9.05 us
    dot_general x1, matrix products, shards(): jnp.einsum('chij,cjhd->cihd', scores, values, preferred_element_type=jnp....  7.57 us
  transfers between devices with their start and end apart: 2, of which 2 were waited for; matrix products, arithmetic and copies ran while one was open for 4% of the time, Pallas kernels for 0%

commit v1 on v0

v1 whole, which is shorter than its diff:
```python
import functools

import jax
import jax.numpy as jnp
from jax import lax
from jax.experimental import pallas as pl
from jax.experimental.pallas import tpu as pltpu
from jax.sharding import PartitionSpec as P

H = 32
DH = 128
BLK = 128
FEAT = H * DH
F32 = jnp.float32
BF16 = jnp.bfloat16
MESH = pl.DeviceIdType.MESH


def silu_round(values):
    half = values.astype(F32) * 0.5
    return (half + half * jnp.tanh(half)).astype(BF16)


def kernel(n, q_hbm, k_hbm, v_hbm, gain_ref, out_ref, fs_ref,
           q_buf, k_buf, v_buf, scores, mixed, sumsq,
           total, first, prefix, x_in, chip, y_in, p_in, p_out, c_out, d_in, d_out,
           q_sem, k_sem, v_sem, x_snd, x_rcv, y_snd, y_rcv, p_snd, p_rcv,
           c_snd, c_rcv, d_snd, d_rcv):
    nz = n // 4
    rows = FEAT // n
    grain = min(rows, DH)
    subs = rows // grain
    steps = n // 2
    heads = 2 * rows // DH
    width = heads * DH
    me = lax.axis_index("ctx")
    grp = lax.axis_index("groups")
    z, y, c = me // 4, (me // 2) % 2, me % 2
    other_core = (grp, me + 1 - 2 * c)
    other_y = (grp, me + 2 - 4 * y)
    above = (grp, me + 4)
    below = (grp, me - 4)
    has_above = z < nz - 1
    has_below = z > 0

    def fetch(hbm, buf, sem, step):
        cols = pl.ds(pl.multiple_of(step * width, width), width)
        return pltpu.make_async_copy(hbm.at[:, cols], buf.at[:, cols], sem.at[step])

    def start_kv(step, _):
        fetch(k_hbm, k_buf, k_sem, step).start()
        fetch(v_hbm, v_buf, v_sem, step).start()
        return 0

    def start_q(step, _):
        fetch(q_hbm, q_buf, q_sem, step).start()
        return 0

    barrier = pltpu.get_barrier_semaphore()
    pl.semaphore_signal(barrier, inc=1, device_id=other_core, device_id_type=MESH)
    pl.semaphore_signal(barrier, inc=1, device_id=other_y, device_id_type=MESH)

    @pl.when(has_above)
    def _():
        pl.semaphore_signal(barrier, inc=1, device_id=above, device_id_type=MESH)

    @pl.when(has_below)
    def _():
        pl.semaphore_signal(barrier, inc=1, device_id=below, device_id_type=MESH)

    lax.fori_loop(0, steps, start_kv, 0)
    lax.fori_loop(0, steps, start_q, 0)

    sumsq[...] = jnp.zeros_like(sumsq)

    @pl.when(z == 0)
    def _():
        p_in[...] = jnp.zeros_like(p_in)

    @pl.when(z == nz - 1)
    def _():
        d_in[...] = jnp.zeros_like(d_in)

    neighbours = 2 + has_above.astype(jnp.int32) + has_below.astype(jnp.int32)
    pl.semaphore_wait(barrier, neighbours)

    def state_rows(step, core, sub):
        return pl.ds(pl.multiple_of((2 * step + core) * rows + sub * grain, grain), grain)

    def half_rows(j):
        return pl.ds(pl.multiple_of(j * grain, grain), grain)

    def remote(src, dst, snd, rcv, device):
        return pltpu.make_async_remote_copy(
            src_ref=src, dst_ref=dst, send_sem=snd, recv_sem=rcv,
            device_id=device, device_id_type=MESH)

    def x_copy(step, sub):
        j = step * subs + sub
        return remote(total.at[state_rows(step, 1 - c, sub)], x_in.at[half_rows(j)],
                      x_snd.at[j], x_rcv.at[j], other_core)

    def y_copy(j):
        return remote(chip.at[half_rows(j)], y_in.at[half_rows(j)],
                      y_snd.at[j], y_rcv.at[j], other_y)

    def p_copy(j):
        return remote(p_out.at[half_rows(j)], p_in.at[half_rows(j)],
                      p_snd.at[j], p_rcv.at[j], above)

    def c_copy(step, sub, core):
        j = step * subs + sub
        return remote(c_out.at[half_rows(j)], prefix.at[state_rows(step, core, sub)],
                      c_snd.at[j], c_rcv.at[j], other_core)

    def d_copy(i):
        return remote(d_out.at[half_rows(i)], d_in.at[half_rows(i)],
                      d_snd.at[i], d_rcv.at[i], below)

    def send_chip(step):
        for sub in range(subs):
            j = step * subs + sub
            x_copy(step, sub).wait_recv()
            chip[half_rows(j), :] = total[state_rows(step, c, sub), :] + x_in[half_rows(j), :]
            y_copy(j).start()

    def states(step, _):
        fetch(k_hbm, k_buf, k_sem, step).wait()
        fetch(v_hbm, v_buf, v_sem, step).wait()
        for a in range(heads):
            head = step * heads + a
            cols = pl.ds(pl.multiple_of(head * DH, DH), DH)
            feat = silu_round(k_buf[:, cols])
            k_buf[:, cols] = feat
            vals = v_buf[:, cols]
            parts = [
                lax.dot_general(feat[b * BLK:(b + 1) * BLK], vals[b * BLK:(b + 1) * BLK],
                                (((0,), (0,)), ((), ())), preferred_element_type=F32)
                for b in range(2)
            ]
            first[cols, :] = parts[0]
            total[cols, :] = parts[0] + parts[1]
        for sub in range(subs):
            x_copy(step, sub).start()

        @pl.when(step > 0)
        def _():
            send_chip(step - 1)

        return 0

    lax.fori_loop(0, steps, states, 0)
    send_chip(steps - 1)

    yf = y.astype(F32)
    cf = c.astype(F32)
    causal = (lax.broadcasted_iota(jnp.int32, (BLK, BLK), 0)
              >= lax.broadcasted_iota(jnp.int32, (BLK, BLK), 1))
    lag = (nz - 1 - z) * 4

    def pass_down(step):
        @pl.when((step >= 0) & (step % 2 == y) & (step // 2 < z))
        def _():
            for sub in range(subs):
                i = (step // 2) * subs + sub
                j = step * subs + sub

                @pl.when(has_above)
                def _():
                    d_copy(i).wait_recv()

                d_out[half_rows(i), :] = (d_in[half_rows(i), :] + chip[half_rows(j), :]
                                          + y_in[half_rows(j), :])
                d_copy(i).start()

    def finish(step):
        for sub in range(subs):
            c_copy(step, sub, 1 - c).wait_recv()
        acc = sumsq[...]
        outs = []
        for a in range(heads):
            head = step * heads + a
            cols = pl.ds(pl.multiple_of(head * DH, DH), DH)
            before = prefix[cols, :]
            carried = [before.astype(BF16), (before + first[cols, :]).astype(BF16)]
            blocks = []
            for b in range(2):
                toks = slice(b * BLK, (b + 1) * BLK)
                left = jnp.concatenate([scores[toks, cols], q_buf[toks, cols]], axis=1)
                right = jnp.concatenate([v_buf[toks, cols], carried[b]], axis=0)
                blocks.append(jnp.dot(left, right, preferred_element_type=F32))
            both = jnp.concatenate(blocks, axis=0)
            mixed[:, cols] = both
            acc = acc + both * both
        sumsq[...] = acc

    def carry(step, _):
        for sub in range(subs):
            j = step * subs + sub
            here = half_rows(j)
            y_copy(j).wait_recv()

            @pl.when(has_below)
            def _():
                p_copy(j).wait_recv()

            arrived = p_in[here, :]
            sibling = y_in[here, :]
            p_out[here, :] = arrived + chip[here, :] + sibling

            @pl.when(has_above)
            def _():
                p_copy(j).start()

            base = arrived + yf * sibling
            mine = state_rows(step, c, sub)
            c_out[here, :] = base + (1.0 - cf) * total[mine, :]
            c_copy(step, sub, c).start()
            prefix[mine, :] = base + cf * x_in[here, :]
        pass_down(step - lag)
        fetch(q_hbm, q_buf, q_sem, step).wait()
        for a in range(heads):
            head = step * heads + a
            cols = pl.ds(pl.multiple_of(head * DH, DH), DH)
            feat = silu_round(q_buf[:, cols])
            q_buf[:, cols] = feat
            for b in range(2):
                toks = slice(b * BLK, (b + 1) * BLK)
                s = lax.dot_general(feat[toks], k_buf[toks, cols],
                                    (((1,), (1,)), ((), ())), preferred_element_type=F32)
                scores[toks, cols] = jnp.where(causal, s, 0.0).astype(BF16)

        @pl.when(step > 0)
        def _():
            finish(step - 1)

        return 0

    lax.fori_loop(0, steps, carry, 0)

    def rest_down(step, _):
        @pl.when(step + lag >= steps)
        def _():
            pass_down(step)

        return 0

    lax.fori_loop(0, steps, rest_down, 0)
    finish(steps - 1)

    scale = lax.rsqrt(jnp.sum(sumsq[...], axis=1, keepdims=True) * (1.0 / FEAT) + 1e-05)

    def normalize(step, _):
        cols = pl.ds(pl.multiple_of(step * width, width), width)
        out_ref[:, cols] = (mixed[:, cols] * scale * gain_ref[:, cols]).astype(BF16)
        return 0

    lax.fori_loop(0, steps, normalize, 0)

    for sub in range(subs):
        @pl.when(has_above)
        def _():
            d_copy(z * subs + sub).wait_recv()

        j = (2 * z + y) * subs + sub
        fs_ref[sub * grain:(sub + 1) * grain, :] = (
            p_out[half_rows(j), :] + d_in[half_rows(z * subs + sub), :]) * (
                (n * q_buf.shape[0]) ** -0.5)

    def drain(step, _):
        for sub in range(subs):
            j = step * subs + sub
            x_copy(step, sub).wait_send()
            y_copy(j).wait_send()

            @pl.when(has_above)
            def _():
                p_copy(j).wait_send()

            c_copy(step, sub, c).wait_send()
        return 0

    lax.fori_loop(0, steps, drain, 0)

    def drain_down(i, _):
        d_copy(i).wait_send()
        return 0

    lax.fori_loop(0, z * subs, drain_down, 0)


def shards(n, query_rows, key_rows, value_rows, out_gain):
    toks = query_rows.shape[0]
    rows = FEAT // n
    grain = min(rows, DH)
    chunks = FEAT // 2 // grain
    downs = (n // 4) * (rows // grain)
    steps = n // 2
    full = pltpu.VMEM((FEAT, DH), F32)
    half = pltpu.VMEM((FEAT // 2, DH), F32)
    down = pltpu.VMEM((downs * grain, DH), F32)
    wide = pltpu.VMEM((toks, FEAT), BF16)
    dma = pltpu.SemaphoreType.DMA
    return pl.pallas_call(
        functools.partial(kernel, n),
        out_shape=(jax.ShapeDtypeStruct((toks, FEAT), BF16),
                   jax.ShapeDtypeStruct((rows, DH), F32)),
        in_specs=[pl.BlockSpec(memory_space=pl.ANY)] * 3
        + [pl.BlockSpec(memory_space=pltpu.VMEM)],
        out_specs=(pl.BlockSpec(memory_space=pltpu.VMEM),
                   pl.BlockSpec(memory_space=pltpu.VMEM)),
        scratch_shapes=[wide] * 4 + [pltpu.VMEM((toks, FEAT), F32), pltpu.VMEM((toks, DH), F32)]
        + [full] * 3 + [half] * 6 + [down] * 2
        + [dma((steps,))] * 3 + [dma((chunks,))] * 8 + [dma((downs,))] * 2,
        compiler_params=pltpu.CompilerParams(
            collective_id=0, has_side_effects=True, vmem_limit_bytes=56 * 1024 * 1024),
        cost_estimate=pl.CostEstimate(
            flops=2 * 4 * toks * FEAT * DH, bytes_accessed=8 * toks * FEAT,
            transcendentals=2 * toks * FEAT),
    )(query_rows, key_rows, value_rows, out_gain.reshape(1, FEAT))


def solution(mesh):
    rows = P(("groups", "ctx"), None)
    return jax.shard_map(
        functools.partial(shards, mesh.shape["ctx"]),
        mesh=mesh,
        in_specs=(rows, rows, rows, P()),
        out_specs=(rows, rows),
        check_vma=False,
    )
```

time: 326 us -> 48 us (0.15)
  waiting for transfers between devices: 218 us -> 0 us
  other arithmetic: 52.3 us -> 0 us
  Pallas kernels: 0 us -> 43.1 us
  matrix products: 18.1 us -> 0 us
  local copies, waits for them, and re-layouts: 20.3 us -> 3.82 us
  between operations: 14.1 us -> 0.65 us
    all_gather x1 -> x0, waiting for transfers between devices: 170 us -> none  [entering(): everything = lax.all_gather(shard, axis)]
    reduce_scatter x1 -> x0, waiting for transfers between devices: 47.1 us -> none  [shards(): lax.psum_scatter(total.reshape(H * DH, DH), 'ctx', scatter_dimension=0, t...]
    pallas_call x0 -> x1, Pallas kernels: none -> 43.1 us  [shards(): pl.pallas_call(functools.partial(kernel, n), out_shape=(jax.ShapeDtypeStr...]
    select_n x16 -> x0, other arithmetic: 37 us -> none  [lap(): return jnp.where(reached, new, before)]
    dot_general x3 -> x0, matrix products: 18.1 us -> none  [the longest x1 9.05 us: shards(): jnp.einsum('cihd,chde->cihe', feat_q, carried, preferred_element_type=jnp...]
    convert_element_type x1 -> x0, other arithmetic: 6.45 us -> none  [shards(): attended = (mixed * scale * out_gain[None, :]).astype(jnp.bfloat16)]
    unnamed x13 -> x4, local copies, waits for them, and re-layouts: 9.87 us -> 3.82 us
    add x1 -> x0, local copies, waits for them, and re-layouts: 5.51 us -> none  [shards(): mixed = (intra + inter).reshape(tok_rows, H * DH)]
  transfers between devices with their start and end apart: 2 -> 0, of which waited for: 2 -> 0; matrix products, arithmetic and copies ran while one was open for 4% -> 0% of each run, Pallas kernels for 0% -> 0%
where the time goes in v1:
time: 48 us; the launch traced here: 47.6 us
  Pallas kernels  43.1 us (90%)
  local copies, waits for them, and re-layouts  3.82 us (8%)
  between operations  0.65 us (1%)
    pallas_call x1, Pallas kernels, shards(): pl.pallas_call(functools.partial(kernel, n), out_shape=(jax.ShapeDtypeStr...  43.1 us
    unnamed x4, local copies, waits for them, and re-layouts  3.82 us

profile of v1, /device:TPU:25, one launch (start us, length us, event | category | flops | bytes accessed | tf_op | source)
XLA Modules:
  0.0 47.6 jit_solution(7015395755816251973)
XLA Ops:
  0.6 43.1 %shard_map.59 = (bf16[256,4096]{1,0:T(8,128)(2,1)}, f32[256,128]{1,0:T(8,128)}) custom-call(bf16[256,4096]{1,0:T(8,128)(2,1)} %q_hbm.1, bf16[256,4096]{1,0:T(8,128)(2,1)} %k_hbm.1, bf16[256,4096]{1,0:T(8,128)(2,1)} %v_hbm.1, f32[1,4096]{1,0:T(1,128)} %bitcast.1), custom_call_target="tpu_custom_call" | custom-call | flops 1073741824 | bytes 8388608 | tf_op jit(solution)/shard_map/pallas_call | solution.py:304
  43.8 0.0 copy-start
  43.8 3.2 %copy.8 = bf16[256,4096]{1,0:T(8,128)(2,1)} copy(bf16[256,4096]{1,0:T(8,128)(2,1)} %get-tuple-element.4) | data formatting | bytes 4194304
  47.0 0.0 copy-done
  47.0 0.7 %copy.9 = f32[256,128]{1,0:T(8,128)} copy(f32[256,128]{1,0:T(8,128)S(1)} %copy-done) | data formatting | bytes 262144
Async XLA Ops:
  43.8 3.2 %copy-start = (f32[256,128]{1,0:T(8,128)S(1)}, f32[256,128]{1,0:T(8,128)}, u32[]{:S(2)}) copy-start(f32[256,128]{1,0:T(8,128)} %get-tuple-element.5) | copy-start | bytes 393220

commit v2 on v1

v2 whole, which is shorter than its diff:
```python
import functools

import jax
import jax.numpy as jnp
from jax import lax
from jax.experimental import pallas as pl
from jax.experimental.pallas import tpu as pltpu
from jax.sharding import PartitionSpec as P

H = 32
DH = 128
BLK = 128
FEAT = H * DH
F32 = jnp.float32
BF16 = jnp.bfloat16
MESH = pl.DeviceIdType.MESH
BEHIND = 2


def silu_round(values):
    half = values.astype(F32) * 0.5
    return (half + half * jnp.tanh(half)).astype(BF16)


def kernel(n, q_hbm, k_hbm, v_hbm, gain_ref, out_ref, fs_ref,
           q_buf, k_buf, v_buf, scores, mixed, sumsq,
           total, first, prefix, x_in, chip, c_out,
           e_in, p_in, p_out, r_in, r_out, d_in, d_out,
           q_sem, k_sem, v_sem, x_snd, x_rcv, c_snd, c_rcv,
           e_snd, e_rcv, p_snd, p_rcv, r_snd, r_rcv, d_snd, d_rcv):
    nz = n // 4
    rows = FEAT // n
    grain = min(rows, DH)
    subs = rows // grain
    steps = n // 2
    heads = 2 * rows // DH
    width = heads * DH
    me = lax.axis_index("ctx")
    grp = lax.axis_index("groups")
    z, y, c = me // 4, (me // 2) % 2, me % 2
    other_core = (grp, me + 1 - 2 * c)
    other_y = (grp, me + 2 - 4 * y)
    above = (grp, me + 4)
    below = (grp, me - 4)
    has_above = z < nz - 1
    has_below = z > 0

    def fetch(hbm, buf, sem, step):
        cols = pl.ds(pl.multiple_of(step * width, width), width)
        return pltpu.make_async_copy(hbm.at[:, cols], buf.at[:, cols], sem.at[step])

    def start_kv(step, _):
        fetch(k_hbm, k_buf, k_sem, step).start()
        fetch(v_hbm, v_buf, v_sem, step).start()
        return 0

    def start_q(step, _):
        fetch(q_hbm, q_buf, q_sem, step).start()
        return 0

    barrier = pltpu.get_barrier_semaphore()
    pl.semaphore_signal(barrier, inc=1, device_id=other_core, device_id_type=MESH)
    pl.semaphore_signal(barrier, inc=1, device_id=other_y, device_id_type=MESH)

    @pl.when(has_above)
    def _():
        pl.semaphore_signal(barrier, inc=1, device_id=above, device_id_type=MESH)

    @pl.when(has_below)
    def _():
        pl.semaphore_signal(barrier, inc=1, device_id=below, device_id_type=MESH)

    lax.fori_loop(0, steps, start_kv, 0)
    lax.fori_loop(0, steps, start_q, 0)

    sumsq[...] = jnp.zeros_like(sumsq)

    @pl.when(z == 0)
    def _():
        p_in[...] = jnp.zeros_like(p_in)

    @pl.when(z == nz - 1)
    def _():
        d_in[...] = jnp.zeros_like(d_in)

    neighbours = 2 + has_above.astype(jnp.int32) + has_below.astype(jnp.int32)
    pl.semaphore_wait(barrier, neighbours)

    def state_rows(piece, core, sub):
        return pl.ds(pl.multiple_of((2 * piece + core) * rows + sub * grain, grain), grain)

    def chunk(j):
        return pl.ds(pl.multiple_of(j * grain, grain), grain)

    def remote(src, dst, snd, rcv, device):
        return pltpu.make_async_remote_copy(
            src_ref=src, dst_ref=dst, send_sem=snd, recv_sem=rcv,
            device_id=device, device_id_type=MESH)

    def x_copy(piece, sub):
        j = piece * subs + sub
        return remote(total.at[state_rows(piece, 1 - c, sub)], x_in.at[chunk(j)],
                      x_snd.at[j], x_rcv.at[j], other_core)

    def e_copy(i):
        j = half_index(i, 1 - y)
        return remote(chip.at[chunk(j)], e_in.at[chunk(i)], e_snd.at[i], e_rcv.at[i], other_y)

    def p_copy(i):
        return remote(p_out.at[chunk(i)], p_in.at[chunk(i)], p_snd.at[i], p_rcv.at[i], above)

    def r_copy(i):
        return remote(r_out.at[chunk(i)], r_in.at[chunk(i)], r_snd.at[i], r_rcv.at[i], other_y)

    def c_copy(i, yy, core):
        j = half_index(i, yy)
        return remote(c_out.at[chunk(j)],
                      prefix.at[state_rows(2 * (i // subs) + yy, core, i % subs)],
                      c_snd.at[j], c_rcv.at[j], other_core)

    def d_copy(i):
        return remote(d_out.at[chunk(i)], d_in.at[chunk(i)], d_snd.at[i], d_rcv.at[i], below)

    def half_index(i, yy):
        return (2 * (i // subs) + yy) * subs + i % subs

    def send_chip(piece):
        for sub in range(subs):
            j = piece * subs + sub
            x_copy(piece, sub).wait_recv()
            chip[chunk(j), :] = total[state_rows(piece, c, sub), :] + x_in[chunk(j), :]

            @pl.when(piece % 2 != y)
            def _():
                e_copy((piece // 2) * subs + sub).start()

    def states(step, _):
        fetch(k_hbm, k_buf, k_sem, step).wait()
        fetch(v_hbm, v_buf, v_sem, step).wait()
        for a in range(heads):
            head = step * heads + a
            cols = pl.ds(pl.multiple_of(head * DH, DH), DH)
            feat = silu_round(k_buf[:, cols])
            k_buf[:, cols] = feat
            vals = v_buf[:, cols]
            parts = [
                lax.dot_general(feat[b * BLK:(b + 1) * BLK], vals[b * BLK:(b + 1) * BLK],
                                (((0,), (0,)), ((), ())), preferred_element_type=F32)
                for b in range(2)
            ]
            first[cols, :] = parts[0]
            total[cols, :] = parts[0] + parts[1]
        for sub in range(subs):
            x_copy(step, sub).start()

        @pl.when(step > 0)
        def _():
            send_chip(step - 1)

        return 0

    lax.fori_loop(0, steps, states, 0)
    send_chip(steps - 1)

    yf = y.astype(F32)
    cf = c.astype(F32)
    causal = (lax.broadcasted_iota(jnp.int32, (BLK, BLK), 0)
              >= lax.broadcasted_iota(jnp.int32, (BLK, BLK), 1))
    count = nz * subs
    lag = (nz - 1 - z) * 4

    def heads_of(i, yy):
        piece = 2 * (i // subs) + yy
        if rows < DH:
            return [piece]
        return [(2 * piece + core) * subs + i % subs for core in range(2)]

    def head_cols(head):
        return pl.ds(pl.multiple_of(head * DH, DH), DH)

    def pass_down(i):
        @pl.when((i >= 0) & (i // subs < z))
        def _():
            @pl.when(has_above)
            def _():
                d_copy(i).wait_recv()

            d_out[chunk(i), :] = (d_in[chunk(i), :] + chip[chunk(half_index(i, y)), :]
                                  + e_in[chunk(i), :])
            d_copy(i).start()

    def share(i, yy, base):
        j = half_index(i, yy)
        mine = state_rows(2 * (i // subs) + yy, c, i % subs)
        c_out[chunk(j), :] = base + (1.0 - cf) * total[mine, :]
        c_copy(i, yy, c).start()
        prefix[mine, :] = base + cf * x_in[chunk(j), :]

    def finish(i, yy):
        c_copy(i, yy, 1 - c).wait_recv()
        acc = sumsq[...]
        for head in heads_of(i, yy):
            cols = head_cols(head)
            before = prefix[cols, :]
            carried = [before.astype(BF16), (before + first[cols, :]).astype(BF16)]
            blocks = []
            for b in range(2):
                toks = slice(b * BLK, (b + 1) * BLK)
                left = jnp.concatenate([scores[toks, cols], q_buf[toks, cols]], axis=1)
                right = jnp.concatenate([v_buf[toks, cols], carried[b]], axis=0)
                blocks.append(jnp.dot(left, right, preferred_element_type=F32))
            both = jnp.concatenate(blocks, axis=0)
            mixed[:, cols] = both
            acc = acc + both * both
        sumsq[...] = acc

    def score(i):
        for yy in range(2):
            for head in heads_of(i, yy):
                cols = head_cols(head)
                feat = silu_round(q_buf[:, cols])
                q_buf[:, cols] = feat
                for b in range(2):
                    toks = slice(b * BLK, (b + 1) * BLK)
                    s = lax.dot_general(feat[toks], k_buf[toks, cols],
                                        (((1,), (1,)), ((), ())), preferred_element_type=F32)
                    scores[toks, cols] = jnp.where(causal, s, 0.0).astype(BF16)

    def carry(i, _):
        @pl.when(i < count)
        def _():
            here = chunk(i)
            e_copy(i).wait_recv()

            @pl.when(has_below)
            def _():
                p_copy(i).wait_recv()

            arrived = p_in[here, :]
            sibling = e_in[here, :]
            own = chip[chunk(half_index(i, y)), :]
            p_out[here, :] = arrived + own + sibling

            @pl.when(has_above)
            def _():
                p_copy(i).start()

            r_out[here, :] = arrived + (1.0 - yf) * own
            r_copy(i).start()
            share(i, y, arrived + yf * sibling)

        back = i - BEHIND

        @pl.when((back >= 0) & (back < count))
        def _():
            r_copy(back).wait_recv()
            share(back, 1 - y, r_in[chunk(back), :])

        @pl.when(i - lag < count)
        def _():
            pass_down(i - lag)

        @pl.when(i < count)
        def _():
            @pl.when(i % subs == 0)
            def _():
                for piece in range(2):
                    fetch(q_hbm, q_buf, q_sem, 2 * (i // subs) + piece).wait()
            score(i)

        @pl.when((i >= 1) & (i - 1 < count))
        def _():
            finish(i - 1, y)

        @pl.when(back >= 1)
        def _():
            finish(back - 1, 1 - y)

        return 0

    trips = count + BEHIND + 1
    lax.fori_loop(0, trips, carry, 0)

    def rest_down(i, _):
        @pl.when(i + lag >= trips)
        def _():
            pass_down(i)

        return 0

    lax.fori_loop(0, count, rest_down, 0)

    scale = lax.rsqrt(jnp.sum(sumsq[...], axis=1, keepdims=True) * (1.0 / FEAT) + 1e-05)

    def normalize(step, _):
        cols = pl.ds(pl.multiple_of(step * width, width), width)
        out_ref[:, cols] = (mixed[:, cols] * scale * gain_ref[:, cols]).astype(BF16)
        return 0

    lax.fori_loop(0, steps, normalize, 0)

    for sub in range(subs):
        i = z * subs + sub

        @pl.when(has_above)
        def _():
            d_copy(i).wait_recv()

        fs_ref[sub * grain:(sub + 1) * grain, :] = (
            p_out[chunk(i), :] + d_in[chunk(i), :]) * ((n * q_buf.shape[0]) ** -0.5)

    def drain(i, _):
        for piece in range(2):
            x_copy(2 * (i // subs) + piece, i % subs).wait_send()
            c_copy(i, piece, c).wait_send()
        e_copy(i).wait_send()
        r_copy(i).wait_send()

        @pl.when(has_above)
        def _():
            p_copy(i).wait_send()

        @pl.when(i // subs < z)
        def _():
            d_copy(i).wait_send()

        return 0

    lax.fori_loop(0, count, drain, 0)


def shards(n, query_rows, key_rows, value_rows, out_gain):
    toks = query_rows.shape[0]
    rows = FEAT // n
    grain = min(rows, DH)
    chunks = FEAT // 2 // grain
    steps = n // 2
    full = pltpu.VMEM((FEAT, DH), F32)
    half = pltpu.VMEM((FEAT // 2, DH), F32)
    quarter = pltpu.VMEM((FEAT // 4, DH), F32)
    wide = pltpu.VMEM((toks, FEAT), BF16)
    dma = pltpu.SemaphoreType.DMA
    return pl.pallas_call(
        functools.partial(kernel, n),
        out_shape=(jax.ShapeDtypeStruct((toks, FEAT), BF16),
                   jax.ShapeDtypeStruct((rows, DH), F32)),
        in_specs=[pl.BlockSpec(memory_space=pl.ANY)] * 3
        + [pl.BlockSpec(memory_space=pltpu.VMEM)],
        out_specs=(pl.BlockSpec(memory_space=pltpu.VMEM),
                   pl.BlockSpec(memory_space=pltpu.VMEM)),
        scratch_shapes=[wide] * 4 + [pltpu.VMEM((toks, FEAT), F32), pltpu.VMEM((toks, DH), F32)]
        + [full] * 3 + [half] * 3 + [quarter] * 7
        + [dma((steps,))] * 3 + [dma((chunks,))] * 4 + [dma((chunks // 2,))] * 8,
        compiler_params=pltpu.CompilerParams(
            collective_id=0, has_side_effects=True, vmem_limit_bytes=56 * 1024 * 1024),
        cost_estimate=pl.CostEstimate(
            flops=2 * 4 * toks * FEAT * DH, bytes_accessed=8 * toks * FEAT,
            transcendentals=2 * toks * FEAT),
    )(query_rows, key_rows, value_rows, out_gain.reshape(1, FEAT))


def solution(mesh):
    rows = P(("groups", "ctx"), None)
    return jax.shard_map(
        functools.partial(shards, mesh.shape["ctx"]),
        mesh=mesh,
        in_specs=(rows, rows, rows, P()),
        out_specs=(rows, rows),
        check_vma=False,
    )
```

time: 48 us -> 47.6 us (level)
  no operation moved by 1% of the time
where the time goes in v2:
time: 47.6 us; the launch traced here: 47.4 us
  Pallas kernels  42.9 us (90%)
  local copies, waits for them, and re-layouts  3.82 us (8%)
  between operations  0.65 us (1%)
    pallas_call x1, Pallas kernels, shards(): pl.pallas_call(functools.partial(kernel, n), out_shape=(jax.ShapeDtypeStr...  42.9 us
    unnamed x4, local copies, waits for them, and re-layouts  3.82 us

profile of v2, /device:TPU:25, one launch (start us, length us, event | category | flops | bytes accessed | tf_op | source)
XLA Modules:
  0.0 47.4 jit_solution(6741236612257684636)
XLA Ops:
  0.6 42.9 %shard_map.59 = (bf16[256,4096]{1,0:T(8,128)(2,1)}, f32[256,128]{1,0:T(8,128)}) custom-call(bf16[256,4096]{1,0:T(8,128)(2,1)} %q_hbm.1, bf16[256,4096]{1,0:T(8,128)(2,1)} %k_hbm.1, bf16[256,4096]{1,0:T(8,128)(2,1)} %v_hbm.1, f32[1,4096]{1,0:T(1,128)} %bitcast.1), custom_call_target="tpu_custom_call" | custom-call | flops 1073741824 | bytes 8388608 | tf_op jit(solution)/shard_map/pallas_call | solution.py:343
  43.6 0.0 copy-start
  43.6 3.2 %copy.8 = bf16[256,4096]{1,0:T(8,128)(2,1)} copy(bf16[256,4096]{1,0:T(8,128)(2,1)} %get-tuple-element.4) | data formatting | bytes 4194304
  46.7 0.0 copy-done
  46.8 0.7 %copy.9 = f32[256,128]{1,0:T(8,128)} copy(f32[256,128]{1,0:T(8,128)S(1)} %copy-done) | data formatting | bytes 262144
Async XLA Ops:
  43.6 3.2 %copy-start = (f32[256,128]{1,0:T(8,128)S(1)}, f32[256,128]{1,0:T(8,128)}, u32[]{:S(2)}) copy-start(f32[256,128]{1,0:T(8,128)} %get-tuple-element.5) | copy-start | bytes 393220

commit v3 on v2

--- a/solution.py
+++ b/solution.py
@@ -14,7 +14,8 @@
 F32 = jnp.float32
 BF16 = jnp.bfloat16
 MESH = pl.DeviceIdType.MESH
-BEHIND = 2
+BEHIND = 3
+SLACK = 2
 
 
 def silu_round(values):
@@ -168,6 +169,7 @@
               >= lax.broadcasted_iota(jnp.int32, (BLK, BLK), 1))
     count = nz * subs
     lag = (nz - 1 - z) * 4
+    behind = BEHIND + SLACK * (nz - 1 - z)
 
     def heads_of(i, yy):
         piece = 2 * (i // subs) + yy
@@ -249,7 +251,7 @@
             r_copy(i).start()
             share(i, y, arrived + yf * sibling)
 
-        back = i - BEHIND
+        back = i - behind
 
         @pl.when((back >= 0) & (back < count))
         def _():
@@ -278,7 +280,7 @@
 
         return 0
 
-    trips = count + BEHIND + 1
+    trips = count + behind + 1
     lax.fori_loop(0, trips, carry, 0)
 
     def rest_down(i, _):
@@ -352,7 +354,7 @@
         + [full] * 3 + [half] * 3 + [quarter] * 7
         + [dma((steps,))] * 3 + [dma((chunks,))] * 4 + [dma((chunks // 2,))] * 8,
         compiler_params=pltpu.CompilerParams(
-            collective_id=0, has_side_effects=True, vmem_limit_bytes=56 * 1024 * 1024),
+            collective_id=0, has_side_effects=True, vmem_limit_bytes=50 * 1024 * 1024),
         cost_estimate=pl.CostEstimate(
             flops=2 * 4 * toks * FEAT * DH, bytes_accessed=8 * toks * FEAT,
             transcendentals=2 * toks * FEAT),

time: 47.6 us -> 38.2 us (0.80)
  Pallas kernels: 42.9 us -> 34.7 us
  local copies, waits for them, and re-layouts: 3.82 us -> 2.69 us
    pallas_call x1, Pallas kernels: 42.9 us -> 34.7 us  [shards(): pl.pallas_call(functools.partial(kernel, n), out_shape=(jax.ShapeDtypeStr...]
    unnamed x4, local copies, waits for them, and re-layouts: 3.82 us -> 2.69 us
where the time goes in v3:
time: 38.2 us; the launch traced here: 38 us
  Pallas kernels  34.7 us (91%)
  local copies, waits for them, and re-layouts  2.69 us (7%)
  between operations  0.65 us (2%)
    pallas_call x1, Pallas kernels, shards(): pl.pallas_call(functools.partial(kernel, n), out_shape=(jax.ShapeDtypeStr...  34.7 us
    unnamed x4, local copies, waits for them, and re-layouts  2.69 us

profile of v3, /device:TPU:25, one launch (start us, length us, event | category | flops | bytes accessed | tf_op | source)
XLA Modules:
  0.0 38.0 jit_solution(15817305875070189519)
XLA Ops:
  0.6 0.0 copy-start
  0.6 0.7 %copy-done = f32[4096]{0:T(1024)S(1)} copy-done((f32[4096]{0:T(1024)S(1)}, f32[4096]{0:T(1024)}, u32[]{:S(2)}) %copy-start) | copy-done | bytes 16408
  1.3 34.7 %shard_map.59 = (bf16[256,4096]{1,0:T(8,128)(2,1)S(1)}, f32[256,128]{1,0:T(8,128)S(1)}) custom-call(bf16[256,4096]{1,0:T(8,128)(2,1)} %q_hbm.1, bf16[256,4096]{1,0:T(8,128)(2,1)} %k_hbm.1, bf16[256,4096]{1,0:T(8,128)(2,1)} %v_hbm.1, f32[1,4096]{1,0:T(1,128)S(1)} %bitcast.1), custom_call_target="tpu_custom_call" | custom-call | flops 1073741824 | bytes 8388608 | tf_op jit(solution)/shard_map/pallas_call | solution.py:345
  36.0 1.3 %copy.8 = bf16[256,4096]{1,0:T(8,128)(2,1)} copy(bf16[256,4096]{1,0:T(8,128)(2,1)S(1)} %get-tuple-element.4) | data formatting | bytes 4194304
  37.3 0.7 %copy.9 = f32[256,128]{1,0:T(8,128)} copy(f32[256,128]{1,0:T(8,128)S(1)} %get-tuple-element.5) | data formatting | bytes 262144
Async XLA Ops:
  0.6 0.7 %copy-start = (f32[4096]{0:T(1024)S(1)}, f32[4096]{0:T(1024)}, u32[]{:S(2)}) copy-start(f32[4096]{0:T(1024)} %param.7) | copy-start | bytes 49156

commit v4 on v3

--- a/solution.py
+++ b/solution.py
@@ -14,7 +14,7 @@
 F32 = jnp.float32
 BF16 = jnp.bfloat16
 MESH = pl.DeviceIdType.MESH
-BEHIND = 3
+BEHIND = 4
 SLACK = 2
 
 
@@ -50,9 +50,13 @@
         cols = pl.ds(pl.multiple_of(step * width, width), width)
         return pltpu.make_async_copy(hbm.at[:, cols], buf.at[:, cols], sem.at[step])
 
+    def piece_at(step):
+        return 2 * (step % nz) + jnp.where(step < nz, 1 - y, y)
+
     def start_kv(step, _):
-        fetch(k_hbm, k_buf, k_sem, step).start()
-        fetch(v_hbm, v_buf, v_sem, step).start()
+        piece = piece_at(step)
+        fetch(k_hbm, k_buf, k_sem, piece).start()
+        fetch(v_hbm, v_buf, v_sem, piece).start()
         return 0
 
     def start_q(step, _):
@@ -85,7 +89,6 @@
         d_in[...] = jnp.zeros_like(d_in)
 
     neighbours = 2 + has_above.astype(jnp.int32) + has_below.astype(jnp.int32)
-    pl.semaphore_wait(barrier, neighbours)
 
     def state_rows(piece, core, sub):
         return pl.ds(pl.multiple_of((2 * piece + core) * rows + sub * grain, grain), grain)
@@ -136,10 +139,11 @@
                 e_copy((piece // 2) * subs + sub).start()
 
     def states(step, _):
-        fetch(k_hbm, k_buf, k_sem, step).wait()
-        fetch(v_hbm, v_buf, v_sem, step).wait()
+        piece = piece_at(step)
+        fetch(k_hbm, k_buf, k_sem, piece).wait()
+        fetch(v_hbm, v_buf, v_sem, piece).wait()
         for a in range(heads):
-            head = step * heads + a
+            head = piece * heads + a
             cols = pl.ds(pl.multiple_of(head * DH, DH), DH)
             feat = silu_round(k_buf[:, cols])
             k_buf[:, cols] = feat
@@ -151,17 +155,21 @@
             ]
             first[cols, :] = parts[0]
             total[cols, :] = parts[0] + parts[1]
+        @pl.when(step == 0)
+        def _():
+            pl.semaphore_wait(barrier, neighbours)
+
         for sub in range(subs):
-            x_copy(step, sub).start()
+            x_copy(piece, sub).start()
 
         @pl.when(step > 0)
         def _():
-            send_chip(step - 1)
+            send_chip(piece_at(step - 1))
 
         return 0
 
     lax.fori_loop(0, steps, states, 0)
-    send_chip(steps - 1)
+    send_chip(piece_at(steps - 1))
 
     yf = y.astype(F32)
     cf = c.astype(F32)

time: 38.2 us -> 37.8 us (0.990)
  Pallas kernels: 34.7 us -> 34.2 us
    pallas_call x1, Pallas kernels: 34.7 us -> 34.2 us  [shards(): pl.pallas_call(functools.partial(kernel, n), out_shape=(jax.ShapeDtypeStr...]
where the time goes in v4:
time: 37.8 us; the launch traced here: 37.5 us
  Pallas kernels  34.2 us (90%)
  local copies, waits for them, and re-layouts  2.69 us (7%)
  between operations  0.65 us (2%)
    pallas_call x1, Pallas kernels, shards(): pl.pallas_call(functools.partial(kernel, n), out_shape=(jax.ShapeDtypeStr...  34.2 us
    unnamed x4, local copies, waits for them, and re-layouts  2.69 us

profile of v4, /device:TPU:25, one launch (start us, length us, event | category | flops | bytes accessed | tf_op | source)
XLA Modules:
  0.0 37.5 jit_solution(3254522288916621737)
XLA Ops:
  0.6 0.0 copy-start
  0.6 0.7 %copy-done = f32[4096]{0:T(1024)S(1)} copy-done((f32[4096]{0:T(1024)S(1)}, f32[4096]{0:T(1024)}, u32[]{:S(2)}) %copy-start) | copy-done | bytes 16408
  1.3 34.2 %shard_map.59 = (bf16[256,4096]{1,0:T(8,128)(2,1)S(1)}, f32[256,128]{1,0:T(8,128)S(1)}) custom-call(bf16[256,4096]{1,0:T(8,128)(2,1)} %q_hbm.1, bf16[256,4096]{1,0:T(8,128)(2,1)} %k_hbm.1, bf16[256,4096]{1,0:T(8,128)(2,1)} %v_hbm.1, f32[1,4096]{1,0:T(1,128)S(1)} %bitcast.1), custom_call_target="tpu_custom_call" | custom-call | flops 1073741824 | bytes 8388608 | tf_op jit(solution)/shard_map/pallas_call | solution.py:353
  35.5 1.3 %copy.8 = bf16[256,4096]{1,0:T(8,128)(2,1)} copy(bf16[256,4096]{1,0:T(8,128)(2,1)S(1)} %get-tuple-element.4) | data formatting | bytes 4194304
  36.9 0.7 %copy.9 = f32[256,128]{1,0:T(8,128)} copy(f32[256,128]{1,0:T(8,128)S(1)} %get-tuple-element.5) | data formatting | bytes 262144
Async XLA Ops:
  0.6 0.7 %copy-start = (f32[4096]{0:T(1024)S(1)}, f32[4096]{0:T(1024)}, u32[]{:S(2)}) copy-start(f32[4096]{0:T(1024)} %param.7) | copy-start | bytes 49156
